TPU v7x, 32 devices: a whole 2x2x4 slice. The times are simulated.
32 devices in a mesh: tower: 2 (over core), rows: 16 (over z, y, x).
Axes of the slice: x: 2, y: 2, z: 4, core: 2. Of those that a mesh axis runs over, the one named last changes fastest.
Arguments:
- tokens: bfloat16 [2, 32, 512, 512], P('tower', 'rows'), may hold values from -9 to 9
- segment_ids: int32 [2, 32, 512], P('tower', 'rows'), may hold values from 0 to 8, never falling along the last dimension, each value on 1 to 128 neighbouring positions
- positives: int32 [256], P('rows'), may hold values from 0 to 255, each once
- attention_gain: float32 [512], replicated, may hold values from 0.5 to 1.5
- query_weight: bfloat16 [512, 512], replicated, may hold values from -0.0625 to 0.0625
- key_weight: bfloat16 [512, 512], replicated, may hold values from -0.25 to 0.25
- value_weight: bfloat16 [512, 512], replicated, may hold values from -0.25 to 0.25
- output_weight: bfloat16 [512, 512], replicated, may hold values from -1 to 1
- position_table: float32 [32, 8], replicated, may hold values from -3 to 3
- feedforward_gain: float32 [512], replicated, may hold values from 0.5 to 1.5
- inner_weight: bfloat16 [512, 2048], replicated, may hold values from -0.25 to 0.25
- outer_weight: bfloat16 [2048, 512], replicated, may hold values from -0.1875 to 0.1875
Outputs:
- layer_output: bfloat16 [2, 32, 512, 512], P('tower', 'rows')
- token_grad: bfloat16 [2, 32, 512, 512], P('tower', 'rows')
- attention_gain_grad: float32 [512], replicated
- query_grad: float32 [512, 512], replicated
- key_grad: float32 [512, 512], replicated
- value_grad: float32 [512, 512], replicated
- output_grad: float32 [512, 512], replicated
- position_grad: float32 [32, 8], replicated
- feedforward_gain_grad: float32 [512], replicated
- inner_grad: float32 [512, 2048], replicated
- outer_grad: float32 [2048, 512], replicated
- contrastive_loss: float32 [], replicated
- root_mean_squares: float32 [3], replicated
Inputs may be any that keep to these rules, and one draw needn't show every extreme that they name: `segment_ids`: within each row of 512 tokens the numbers never fall; 0 to 7 are the row's items and 8 marks the padding at its end; every number, padding included, covers 1 to 128 tokens. positives[m] is the document item paired with query item m; every document item occurs once.
All inputs are finite; a program needn't handle non-finite values.
Results may differ from a plain program's by a relative error of at most 0.028.
The roundings to bfloat16 on the way count: a program that leaves them out, or rounds other values in their place, can miss the bound.
Values sent between devices are 32-bit elements; how exact they have to be, the bound alone decides.
A program may use at most 320 MiB of HBM per device.

v0:
```python
import math

import jax
import jax.numpy as jnp
import numpy as np
from jax import lax
from jax.sharding import PartitionSpec as P

MAX_DIST = 128
ITEMS_ROW = 8


EPSILON = 1e-06
SOFTMAX_TEMP = 0.01
LOSS_SCALE = 65536.0
MATMUL_PRECISION = lax.Precision.HIGHEST


def from_partner(value, axis, apart):
    mask = 2**apart
    pairs = [(source, source ^ mask) for source in range(lax.axis_size(axis))]
    return lax.ppermute(value, axis, pairs)


def bucket_table(length, bucket_count, far_limit):
    half_count = bucket_count // 2
    exact_count = half_count // 2
    entries = []
    for offset in range(1 - length, length):
        distance = abs(offset)
        if distance < exact_count:
            within = distance
        else:
            within = exact_count + int(
                math.log(distance / exact_count)
                / math.log(far_limit / exact_count)
                * (half_count - exact_count)
            )
            within = min(within, half_count - 1)
        entries.append(within + (half_count if offset > 0 else 0))
    by_offset = np.array(entries, dtype=np.int32)
    index_grid = np.arange(length)[None, :] - np.arange(length)[:, None] + length - 1
    return (by_offset, by_offset[index_grid])


def contract_rows(left_side, right_side):
    return lax.dot_general(
        left_side, right_side, (((0,), (0,)), ((), ())), preferred_element_type=jnp.float32
    )


def times_transpose(left_side, right_side):
    return lax.dot_general(
        left_side, right_side, (((1,), (1,)), ((), ())), preferred_element_type=jnp.float32
    )


def norm_scale(values):
    return lax.rsqrt(jnp.mean(values * values, axis=1, keepdims=True) + EPSILON)


def norm_back(grad_normed, values, scale, gain):
    gained = grad_normed * gain
    return scale * (
        gained - values * scale * scale * jnp.mean(gained * values, axis=1, keepdims=True)
    )


def row_scores(query_part, key_part, segment_row, position_bias, head_count):
    length = query_part.shape[0]
    query_heads = query_part.reshape(length, head_count, -1)
    key_heads = key_part.reshape(length, head_count, -1)
    scores = (
        jnp.einsum("qhd,khd->hqk", query_heads, key_heads, preferred_element_type=jnp.float32)
        + position_bias
    )
    same_item = segment_row[:, None] == segment_row[None, :]
    return jnp.where(same_item[None], scores, -1e30)


def diagonal_sums(square):
    head_count = square.shape[0]
    length = square.shape[1]
    flipped = square[:, :, ::-1]
    padded = jnp.pad(flipped, ((0, 0), (0, 0), (0, length)))
    sheared = padded.reshape(head_count, 2 * length * length)[:, : length * (2 * length - 1)]
    sheared = sheared.reshape(head_count, length, 2 * length - 1)
    return jnp.sum(sheared, axis=1)[:, ::-1]


def shards(
    tokens,
    segment_ids,
    positives,
    attention_gain,
    query_weight,
    key_weight,
    value_weight,
    output_weight,
    position_table,
    feedforward_gain,
    inner_weight,
    outer_weight,
):
    row_count = tokens.shape[1]
    length = tokens.shape[2]
    model_width = tokens.shape[3]
    head_count = position_table.shape[1]
    inner_width = query_weight.shape[1]
    head_size = inner_width // head_count
    token_count = row_count * length
    by_offset, bucket_index = bucket_table(length, position_table.shape[0], MAX_DIST)
    position_bias = jnp.take(position_table.T, jnp.asarray(bucket_index), axis=1)
    inputs = tokens.reshape(token_count, model_width).astype(jnp.float32)
    segments = segment_ids.reshape(row_count, length)
    scale_one = norm_scale(inputs)
    normed_one = (inputs * scale_one * attention_gain).astype(jnp.bfloat16)
    query_rows = jnp.dot(normed_one, query_weight, preferred_element_type=jnp.float32).astype(
        jnp.bfloat16
    )
    key_rows = jnp.dot(normed_one, key_weight, preferred_element_type=jnp.float32).astype(
        jnp.bfloat16
    )
    value_rows = jnp.dot(normed_one, value_weight, preferred_element_type=jnp.float32).astype(
        jnp.bfloat16
    )
    query_blocks = query_rows.reshape(row_count, length, inner_width)
    key_blocks = key_rows.reshape(row_count, length, inner_width)
    value_blocks = value_rows.reshape(row_count, length, inner_width)

    def attend(packed):
        query_part, key_part, value_part, segment_row = packed
        scores = row_scores(query_part, key_part, segment_row, position_bias, head_count)
        highest = jnp.max(scores, axis=2, keepdims=True)
        exp_scores = jnp.exp(scores - highest)
        exp_total = jnp.sum(exp_scores, axis=2, keepdims=True)
        attention_probs = (exp_scores / exp_total).astype(jnp.bfloat16)
        value_heads = value_part.reshape(length, head_count, head_size)
        mixed_heads = jnp.einsum(
            "hqk,khd->qhd", attention_probs, value_heads, preferred_element_type=jnp.float32
        )
        return (
            mixed_heads.reshape(length, inner_width).astype(jnp.bfloat16),
            (highest + jnp.log(exp_total))[:, :, 0],
        )

    mixed_blocks, log_totals = lax.map(attend, (query_blocks, key_blocks, value_blocks, segments))
    mixed_rows = mixed_blocks.reshape(token_count, inner_width)
    branch_one = jnp.dot(mixed_rows, output_weight, preferred_element_type=jnp.float32)
    middle = inputs + branch_one
    scale_two = norm_scale(middle)
    normed_two = (middle * scale_two * feedforward_gain).astype(jnp.bfloat16)
    hidden = jax.nn.relu(
        jnp.dot(normed_two, inner_weight, preferred_element_type=jnp.float32)
    ).astype(jnp.bfloat16)
    branch_two = jnp.dot(hidden, outer_weight, preferred_element_type=jnp.float32)
    result = middle + branch_two
    valid_mask = (segments < ITEMS_ROW).astype(jnp.float32).reshape(token_count, 1)
    stat_terms = jnp.stack(
        [
            jnp.sum(valid_mask * result * result),
            jnp.sum(valid_mask * branch_one * branch_one),
            jnp.sum(valid_mask * branch_two * branch_two),
            jnp.sum(valid_mask),
        ]
    )
    stat_totals = lax.psum(stat_terms, ("tower", "rows"))
    member = (segments[:, None, :] == jnp.arange(ITEMS_ROW)[None, :, None]).astype(jnp.float32)
    item_sizes = jnp.sum(member, axis=2, keepdims=True)
    result_blocks = result.reshape(row_count, length, model_width)
    pooled = (
        jnp.einsum("ris,rsd->rid", member, result_blocks, precision=MATMUL_PRECISION) / item_sizes
    )
    items_here = row_count * ITEMS_ROW
    pooled = pooled.reshape(items_here, model_width)
    inverse_norm = lax.rsqrt(jnp.sum(pooled * pooled, axis=1, keepdims=True) + EPSILON)
    embedded_tokens = pooled * inverse_norm
    tower_index = lax.axis_index("tower")
    is_query = tower_index == 0
    partner = from_partner(embedded_tokens, "tower", 0)
    query_vectors = jnp.where(is_query, embedded_tokens, partner)
    document_vectors = jnp.where(is_query, partner, embedded_tokens)
    gathered_documents = lax.all_gather(document_vectors, "rows", axis=0, tiled=True)
    item_total = gathered_documents.shape[0]
    half_items = items_here // 2
    my_queries = lax.dynamic_slice_in_dim(query_vectors, tower_index * half_items, half_items, 0)
    my_targets = lax.dynamic_slice_in_dim(positives, tower_index * half_items, half_items, 0)
    similarity_scores = (
        lax.dot_general(
            my_queries,
            gathered_documents,
            (((1,), (1,)), ((), ())),
            precision=MATMUL_PRECISION,
            preferred_element_type=jnp.float32,
        )
        / SOFTMAX_TEMP
    )
    highest = jnp.max(similarity_scores, axis=1, keepdims=True)
    exp_logits = jnp.exp(similarity_scores - highest)
    exp_total = jnp.sum(exp_logits, axis=1, keepdims=True)
    log_total = highest[:, 0] + jnp.log(exp_total[:, 0])
    is_target = jnp.arange(item_total)[None, :] == my_targets[:, None]
    target = jnp.sum(jnp.where(is_target, similarity_scores, 0.0), axis=1)
    loss_part = jnp.sum(log_total - target)
    similarity_gradient = (exp_logits / exp_total - is_target.astype(jnp.float32)) * (
        LOSS_SCALE / item_total
    )
    local_gradient = (
        jnp.dot(similarity_gradient, gathered_documents, precision=MATMUL_PRECISION) / SOFTMAX_TEMP
    )
    grad_documents = lax.psum_scatter(
        lax.dot_general(
            similarity_gradient,
            my_queries,
            (((0,), (0,)), ((), ())),
            precision=MATMUL_PRECISION,
            preferred_element_type=jnp.float32,
        )
        / SOFTMAX_TEMP,
        "rows",
        scatter_dimension=0,
        tiled=True,
    )
    partner_mine, partner_documents = from_partner((local_gradient, grad_documents), "tower", 0)
    query_side = jnp.where(
        is_query,
        jnp.concatenate([local_gradient, partner_mine], 0),
        jnp.concatenate([partner_mine, local_gradient], 0),
    )
    own_grad = jnp.where(is_query, query_side, grad_documents + partner_documents)
    inner_along = jnp.sum(own_grad * embedded_tokens, axis=1, keepdims=True)
    grad_pooled = inverse_norm * (own_grad - embedded_tokens * inner_along)
    per_token = grad_pooled.reshape(row_count, ITEMS_ROW, model_width) / item_sizes
    grad_result = jnp.einsum("ris,rid->rsd", member, per_token, precision=MATMUL_PRECISION).reshape(
        token_count, model_width
    )
    grad_branch_two = grad_result.astype(jnp.bfloat16)
    outer_grad = contract_rows(hidden, grad_branch_two)
    grad_hidden = times_transpose(grad_branch_two, outer_weight)
    grad_pre = jnp.where(hidden > 0, grad_hidden, 0.0).astype(jnp.bfloat16)
    inner_grad = contract_rows(normed_two, grad_pre)
    grad_normed_two = times_transpose(grad_pre, inner_weight)
    feedforward_gain_grad = jnp.sum(grad_normed_two * middle * scale_two, axis=0)
    grad_middle = grad_result + norm_back(grad_normed_two, middle, scale_two, feedforward_gain)
    grad_branch_one = grad_middle.astype(jnp.bfloat16)
    output_grad = contract_rows(mixed_rows, grad_branch_one)
    grad_mixed = times_transpose(grad_branch_one, output_weight).astype(jnp.bfloat16)
    grad_mixed_blocks = grad_mixed.reshape(row_count, length, inner_width)

    def attend_back(running, packed):
        query_part, key_part, value_part, segment_row, row_log_total, grad_part = packed
        scores = row_scores(query_part, key_part, segment_row, position_bias, head_count)
        attention_probs = jnp.exp(scores - row_log_total[:, :, None])
        query_heads = query_part.reshape(length, head_count, head_size)
        key_heads = key_part.reshape(length, head_count, head_size)
        value_heads = value_part.reshape(length, head_count, head_size)
        grad_heads = grad_part.reshape(length, head_count, head_size)
        grad_value = jnp.einsum(
            "hqk,qhd->khd",
            attention_probs.astype(jnp.bfloat16),
            grad_heads,
            preferred_element_type=jnp.float32,
        )
        grad_probs = jnp.einsum(
            "qhd,khd->hqk", grad_heads, value_heads, preferred_element_type=jnp.float32
        )
        row_dot = jnp.sum(attention_probs * grad_probs, axis=2, keepdims=True)
        grad_scores = (attention_probs * (grad_probs - row_dot)).astype(jnp.bfloat16)
        grad_query = jnp.einsum(
            "hqk,khd->qhd", grad_scores, key_heads, preferred_element_type=jnp.float32
        )
        grad_key = jnp.einsum(
            "hqk,qhd->khd", grad_scores, query_heads, preferred_element_type=jnp.float32
        )
        outputs = (
            grad_query.reshape(length, inner_width).astype(jnp.bfloat16),
            grad_key.reshape(length, inner_width).astype(jnp.bfloat16),
            grad_value.reshape(length, inner_width).astype(jnp.bfloat16),
        )
        return (running + grad_scores.astype(jnp.float32), outputs)

    score_sum, grad_rows = lax.scan(
        attend_back,
        jnp.zeros((head_count, length, length), jnp.float32),
        (query_blocks, key_blocks, value_blocks, segments, log_totals, grad_mixed_blocks),
    )
    grad_queries = grad_rows[0].reshape(token_count, inner_width)
    grad_keys = grad_rows[1].reshape(token_count, inner_width)
    grad_values = grad_rows[2].reshape(token_count, inner_width)
    query_grad = contract_rows(normed_one, grad_queries)
    key_grad = contract_rows(normed_one, grad_keys)
    value_grad = contract_rows(normed_one, grad_values)
    grad_normed_one = (
        times_transpose(grad_queries, query_weight)
        + times_transpose(grad_keys, key_weight)
        + times_transpose(grad_values, value_weight)
    )
    attention_gain_grad = jnp.sum(grad_normed_one * inputs * scale_one, axis=0)
    token_grad = grad_middle + norm_back(grad_normed_one, inputs, scale_one, attention_gain)
    offset_onehot = jnp.asarray(
        (by_offset[:, None] == np.arange(position_table.shape[0])[None, :]).astype(np.float32)
    )
    position_grad = jnp.dot(diagonal_sums(score_sum), offset_onehot, precision=MATMUL_PRECISION).T
    closing_terms = loss_part[None]
    summed = lax.psum(
        (
            attention_gain_grad,
            query_grad,
            key_grad,
            value_grad,
            output_grad,
            position_grad,
            feedforward_gain_grad,
            inner_grad,
            outer_grad,
            closing_terms,
        ),
        ("tower", "rows"),
    )
    (
        attention_gain_grad,
        query_grad,
        key_grad,
        value_grad,
        output_grad,
        position_grad,
        feedforward_gain_grad,
        inner_grad,
        outer_grad,
        closing_totals,
    ) = summed
    contrastive_loss = closing_totals[0] / item_total
    root_mean_squares = jnp.sqrt(stat_totals[:3] / (stat_totals[3] * model_width))
    block_shape = (1, row_count, length, model_width)
    return (
        result.reshape(block_shape).astype(jnp.bfloat16),
        token_grad.reshape(block_shape).astype(jnp.bfloat16),
        attention_gain_grad,
        query_grad,
        key_grad,
        value_grad,
        output_grad,
        position_grad,
        feedforward_gain_grad,
        inner_grad,
        outer_grad,
        contrastive_loss,
        root_mean_squares,
    )


def solution(mesh):
    return jax.shard_map(
        shards,
        mesh=mesh,
        in_specs=(
            P("tower", "rows", None, None),
            P("tower", "rows", None),
            P("rows"),
            P(),
            P(),
            P(),
            P(),
            P(),
            P(),
            P(),
            P(),
            P(),
        ),
        out_specs=(
            P("tower", "rows", None, None),
            P("tower", "rows", None, None),
            P(),
            P(),
            P(),
            P(),
            P(),
            P(),
            P(),
            P(),
            P(),
            P(),
            P(),
        ),
        check_vma=False,
    )
```

profile of v0, /device:TPU:0, one launch (start us, length us, event | category | flops | bytes accessed | tf_op | source)
XLA Modules:
  0.0 1486.6 jit_solution(8252469070416313084)
XLA Ops:
  12.8 2.3 copy.46
  15.0 2.7 convolution_convert_fusion.4
  17.8 2.3 copy.47
  20.0 2.7 convolution_convert_fusion.3
  22.7 2.3 copy.48
  26.5 865.7 %gather_fusion = f32[262144,8]{1,0:T(8,128)} fusion(f32[8,32]{0,1:T(8,128)S(1)} %bitcast.203, s32[262144]{0:T(1024)S(1)} %broadcast_clamp_fusion), kind=kCustom, calls=%fused_computation | custom fusion | bytes 17825792 | tf_op jit(solution)/shard_map/jit(_take)/gather | solution.py:113
  892.2 70.9 %copy.45 = f32[512,512,8]{0,1,2:T(8,128)} copy(f32[512,512,8]{2,1,0:T(8,128)} %bitcast.13) | data formatting | bytes 16777216 | tf_op jit(solution)/shard_map/jit(_take)/gather | solution.py:113
  964.2 23.2 %while.29 = (s32[]{:T(128)}, bf16[2,512,512]{2,1,0:T(8,128)(2,1)}, f32[2,8,512]{2,1,0:T(8,128)S(1)}, bf16[2,512,512]{1,2,0:T(8,128)(2,1)}, s32[2,512]{1,0:T(2,12...) while((s32[]{:T(128)}, bf16[2,512,512]{2,1,0:T(8,128)(2,1)}, ...), condition=%wide.region_4.5_spmd, body=%wide.region_1.0_spmd.sunk | while | flops 554168320 | bytes 41556588 | solution.py:147
  965.7 5.0 fusion.126
  977.1 5.0 fusion.126
  987.4 2.5 multiply_reduce_fusion.3
  990.0 2.4 maximum_convert_fusion
  992.4 3.4 fusion.8
  999.7 45.4 %all_gather.3 = f32[256,512]{1,0:T(8,128)S(1)} all-gather(f32[16,512]{1,0:T(8,128)S(1)} %broadcast_select_fusion), channel_id=1, replica_groups=mesh['tower'=2,'rows'=16] {'rows'}, dimensions={0}, use_global_device_ids=true | all-gather | bytes 557056 | tf_op jit(solution)/shard_map/all_gather | solution.py:183
  1050.5 70.9 %reduce-scatter.2.cloned.1.call-done = f32[16,512]{1,0:T(8,128)} async-done(((f32[256,512]{1,0:T(8,128)}), f32[16,512]{1,0:T(8,128)}) %reduce-scatter.2.cloned.1.call-update) | async-done | bytes 32784 | tf_op jit(solution)/shard_map/reduce_scatter | solution.py:211
  1125.7 4.7 select_convert_fusion
  1130.4 4.5 fusion.56
  1134.9 3.1 multiply_reduce_fusion.1
  1138.0 4.6 fusion.44
  1150.8 74.2 %while.30 = (s32[]{:T(128)}, f32[8,512,512]{1,2,0:T(8,128)}, bf16[2,512,512]{2,1,0:T(8,128)(2,1)}, bf16[2,512,512]{2,1,0:T(8,128)(2,1)}, bf16[2,512,512]{2,1,0:T...) while((s32[]{:T(128)}, f32[8,512,512]{1,2,0:T(8,128)}, ...), condition=%wide.region_15.16_spmd.clone, body=%wide.region_13.15_spmd.clone.sunk | while | flops 1368387584 | bytes 197745472 | solution.py:282
  1153.4 3.4 constant_dynamic-slice_fusion.22
  1156.8 1.9 constant_dynamic-slice_fusion.23
  1159.0 5.0 multiply_reduce_fusion.7
  1164.0 9.8 select_add_fusion.2
  1175.9 4.8 fusion.140
  1182.0 3.1 convolution_convert_fusion.8
  1189.0 3.4 constant_dynamic-slice_fusion.22
  1194.6 5.0 multiply_reduce_fusion.7
  1199.5 13.0 select_add_fusion.2
  1214.7 4.8 fusion.140
  1220.7 3.1 convolution_convert_fusion.8
  1225.0 3.4 fusion.53
  1235.1 2.7 pad_maximum_fusion
  1238.4 64.3 %rev.6 = f32[8,512,512]{1,2,0:T(8,128)} reverse(f32[8,512,512]{1,2,0:T(8,128)} %get-tuple-element.126), dimensions={2} | reverse | bytes 16777216 | tf_op jit(solution)/shard_map/rev | solution.py:84
  1302.7 9.7 copy.71
  1312.4 11.6 pad_bitcast_fusion
  1324.0 15.5 %copy.73 = f32[1,8,512,1024]{3,1,2,0:T(8,128)S(1)} copy(f32[1,8,512,1024]{3,2,1,0:T(8,128)} %pad_bitcast_fusion) | data formatting | bytes 33554432
  1339.5 6.0 slice.14
  1345.5 13.0 reshape.408
  1358.4 17.6 %reshape.392 = f32[8,512,1023]{2,1,0:T(8,128)} reshape(f32[4190208]{0:T(1024)} %reshape.408) | data formatting | bytes 33521664 | tf_op jit(solution)/shard_map/reshape | solution.py:87
  1376.1 7.4 reduce_sum.180
  1386.9 2.5 fusion.24
  1389.4 38.0 %all-reduce.1 = (f32[512]{0:T(512)}, f32[32,8]{0,1:T(8,128)}, f32[512]{0:T(512)}, f32[1]{0:T(128)}, f32[4]{0:T(128)S(1)}) all-reduce(f32[512]{0:T(512)S(1)} %get-tuple-element.208, f32[32,8]{0,1:T(8,128)S(1)} %fusion.48, f32[512]{0:T(512)S(1)} %copy-done.46, f32[1]{0:T(128)} %bitcast.27, ...), channel_id=1, replica_groups=mesh['tower'=2,'rows'=16] {'tower','rows'}, use_global_device_ids=true, to_apply=%region_18.19 | all-reduce | flops 1285 | bytes 10280 | tf_op jit(solution)/shard_map/psum | solution.py:305
  1429.8 4.1 fusion.18
  1434.0 31.9 %all-reduce.5.cloned.1.call-done = (f32[512,512]{1,0:T(8,128)}, f32[512,512]{1,0:T(8,128)}, f32[512,512]{1,0:T(8,128)}, f32[512,512]{1,0:T(8,128)}, f32[512,2048]{1,0:T(8,128)}, /*index=5*/f32[2048,512]{1,0:T(8,128)}) async-done(((f32[512,512]{1,0:T(8,128)}, f32[512,512]{1,0:T(8,128)}, f32[512,512]{1,0:T(8,128)}, f32[512,512]{1,0:T(8,128)}, f32[512,2048]{1,0:T(8,128)}, /*index=5*/f32[2048,512]{1,0:T(8,128)}), ...) | async-done | bytes 12582928 | tf_op jit(solution)/shard_map/psum | solution.py:305
  1465.9 2.4 copy.120
  1471.4 2.1 copy.124
  1475.1 2.1 copy.125
  (219 shorter events, 76.8 us)
Async XLA Ops:
  7.2 982.8 %copy-start = (bf16[512,2048]{1,0:T(8,128)(2,1)S(1)}, bf16[512,2048]{1,0:T(8,128)(2,1)}, u32[]{:S(2)}) copy-start(bf16[512,2048]{1,0:T(8,128)(2,1)} %param.28) | copy-start | bytes 6291460
  7.2 1114.2 %reduce-scatter.2.cloned.1.call-start = ((), (), s32[]{:S(2)}) async-start(), calls=%async_computation.1 | async-start | bytes 557056 | tf_op jit(solution)/shard_map/reduce_scatter | solution.py:211
  7.2 3.8 copy-start.29
  9.5 3.2 copy-start.33
  22.7 3.7 copy-start.44
  892.2 70.9 %copy-start.32 = (s32[1,2,512]{2,1,0:T(2,128)S(1)}, s32[1,2,512]{2,1,0:T(2,128)}, u32[]{:S(2)}) copy-start(s32[1,2,512]{2,1,0:T(2,128)} %param.19) | copy-start | bytes 12292
  987.4 2.6 copy-start.38
  989.9 2.5 copy-start.8
  990.0 2.4 copy-start.47
  992.4 3.5 copy-start.50
  995.9 2.9 copy-start.49
  997.2 124.2 %copy-start.5 = (bf16[1,2,512,512]{3,2,1,0:T(8,128)(2,1)S(1)}, bf16[1,2,512,512]{3,2,1,0:T(8,128)(2,1)}, u32[]{:S(2)}) copy-start(bf16[1,2,512,512]{3,2,1,0:T(8,128)(2,1)} %param.18) | copy-start | bytes 3145732
  997.2 124.2 %copy-start.35 = (f32[512]{0:T(512)S(1)}, f32[512]{0:T(512)}, u32[]{:S(2)}) copy-start(f32[512]{0:T(512)} %param.21) | copy-start | bytes 6148
  997.2 124.2 %copy-start.39 = (f32[2,512]{1,0:T(2,128)S(1)}, f32[2,512]{1,0:T(2,128)}, u32[]{:S(2)}) copy-start(f32[2,512]{1,0:T(2,128)} %get-tuple-element.281) | copy-start | bytes 12292
  998.3 1.3 collective-permute-start
  1046.5 4.0 copy-start.40
  1047.3 3.2 copy-start.42
  1048.9 417.0 %all-reduce.5.cloned.1.call-start = ((), (), s32[]{:S(2)}) async-start(), calls=%async_computation.2 | async-start | bytes 25165824 | tf_op jit(solution)/shard_map/psum | solution.py:305
  1050.5 72.2 %collective-permute-start.1 = (f32[8,512]{1,0:T(8,128)S(1)}, f32[8,512]{1,0:T(8,128)S(1)}, u32[]{:S(2)}, u32[]{:S(2)}) collective-permute-start(f32[8,512]{1,0:T(8,128)S(1)} %convolution_multiply_fusion.1), channel_id=1, source_target_pairs={{0,16},{16,0},{1,17},{17,1},{2,18},{18,2},{3,19},{19,3},{4,20},{20... | collective-permute-start | bytes 49160 | tf_op jit(solution)/shard_map/ppermute | solution.py:22
  1121.4 1.4 collective-permute-start.2
  1125.7 4.7 copy-start.51
  1130.4 4.5 copy-start.9
  1143.7 3.8 copy-start.7
  1143.7 2.0 copy-start.10
  1152.1 6.9 copy-start.3
  1153.4 10.6 copy-start.2
  1173.8 1.9 copy-start.4
  1182.0 3.3 copy-start.14
  1187.6 6.9 copy-start.3
  1188.9 10.6 copy-start.2
  1212.5 1.9 copy-start.4
  1220.7 3.3 copy-start.14
  1225.0 3.4 copy-start.17
  1225.0 3.4 copy-start.23
  1228.4 1.7 copy-start.18
  1233.4 4.4 copy-start.41
  1233.4 4.4 copy-start.43
  1233.4 4.4 copy-start.45
  1376.1 8.0 copy-start.31
  1376.1 8.4 copy-start.16
  1376.1 8.4 copy-start.27
  1386.9 2.5 copy-start.46
  1465.9 2.4 copy-start.26
  1465.9 3.4 copy-start.25
  1465.9 4.4 copy-start.24
  1468.3 3.1 copy-start.21
  1471.4 3.7 copy-start.20
  1475.1 3.1 copy-start.1
  (14 other events, 18.7 us)
Sparse Core Ops, SparseCore 0:
  1049.0 72.3 reduce-scatter.1
  1232.0 233.8 all-reduce.4
where the time goes:
time: 1500 us; the launch traced here: 1490 us
  local copies, waits for them, and re-layouts  1130 us (75%)
  waiting for transfers between devices  104 us (7%)
  matrix products  95.6 us (6%)
  blocking collectives  83.4 us (6%)
  other arithmetic  51.3 us (3%)
  between operations  17.3 us (1%)
    gather x2, local copies, waits for them, and re-layouts, shards(): jnp.take(position_table.T, jnp.asarray(bucket_index), axis=1)  937 us
    reduce_scatter x1, waiting for transfers between devices, shards(): lax.psum_scatter(lax.dot_general(similarity_gradient, my_queries, (((0,),...  70.9 us
    unnamed x108, local copies, waits for them, and re-layouts  70.6 us
    rev x1, local copies, waits for them, and re-layouts, diagonal_sums(): flipped = square[:, :, ::-1]  64.3 us
    all_gather x1, blocking collectives, shards(): lax.all_gather(document_vectors, 'rows', axis=0, tiled=True)  45.4 us
    psum x1, blocking collectives, shards(): lax.psum((attention_gain_grad, query_grad, key_grad, value_grad, output_g...  38 us
    psum x1, waiting for transfers between devices, shards(): lax.psum((attention_gain_grad, query_grad, key_grad, value_grad, output_g...  31.9 us
  transfers between devices with their start and end apart: 5, of which 4 were waited for; matrix products, arithmetic and copies ran while one was open for 11% of the time, Pallas kernels for 0%

commit v1 on v0

--- a/solution.py
+++ b/solution.py
@@ -1,9 +1,12 @@
+import functools
 import math
 
 import jax
 import jax.numpy as jnp
 import numpy as np
 from jax import lax
+from jax.experimental import pallas as pl
+from jax.experimental.pallas import tpu as pltpu
 from jax.sharding import PartitionSpec as P
 
 MAX_DIST = 128
@@ -349,9 +352,911 @@
     )
 
 
+F32 = jnp.float32
+BF = jnp.bfloat16
+MESH = pl.DeviceIdType.MESH
+NN = (((1,), (0,)), ((), ()))
+NT = (((1,), (1,)), ((), ()))
+TN = (((0,), (0,)), ((), ()))
+UNITS = 16
+HALVES = (256, 128, 64, 32, 16)
+OFFSETS = (0, 256, 384, 448, 480)
+FAR = 768
+NEAR = 640
+
+
+def dot(a, b, dims=NN):
+    return lax.dot_general(a, b, dims, preferred_element_type=F32)
+
+
+def exact_dot(a, b, dims=NN):
+    return lax.dot_general(
+        a, b, dims, precision=lax.Precision.HIGHEST, preferred_element_type=F32
+    )
+
+
+def tile(index, size):
+    return pl.ds(pl.multiple_of(index * size, size), size)
+
+
+def far_limits(bucket_count, far_limit):
+    half_count = bucket_count // 2
+    exact_count = half_count // 2
+    limits = []
+    reached = exact_count
+    for distance in range(exact_count, 512):
+        within = exact_count + int(
+            math.log(distance / exact_count)
+            / math.log(far_limit / exact_count)
+            * (half_count - exact_count)
+        )
+        within = min(within, half_count - 1)
+        while reached < within:
+            limits.append(distance)
+            reached += 1
+    return limits
+
+
+def bucket_onehot(offset):
+    distance = jnp.abs(offset)
+    far = jnp.full_like(distance, 8)
+    for limit in far_limits(32, MAX_DIST):
+        far = far + jnp.where(distance >= limit, 1, 0)
+    bucket = jnp.where(distance < 8, distance, far) + jnp.where(offset > 0, 16, 0)
+    same = bucket == lax.broadcasted_iota(jnp.int32, (32, FAR), 0)
+    return jnp.where(same, 1.0, 0.0).astype(F32)
+
+
+def split_three(value):
+    high = value.astype(BF)
+    rest = value - high.astype(F32)
+    middle = rest.astype(BF)
+    return high, middle, (rest - middle.astype(F32)).astype(BF)
+
+
+class Place:
+    def __init__(self):
+        self.tower = lax.axis_index("tower")
+        self.rows = lax.axis_index("rows")
+        self.flat = lax.rem(self.rows, 4)
+        self.deep = lax.div(self.rows, 4)
+        bits = {
+            "x": lax.rem(self.rows, 2),
+            "y": lax.rem(lax.div(self.rows, 2), 2),
+            "z": lax.rem(lax.div(self.rows, 4), 2),
+            "w": lax.div(self.rows, 8),
+        }
+        steps = {"x": 1, "y": 2, "z": 4, "w": 8}
+        self.bit = {"c": self.tower, **bits}
+        self.to = {"c": self.device(1 - self.tower, self.rows)}
+        for name, step in steps.items():
+            self.to[name] = self.device(self.tower, self.rows + step * (1 - 2 * bits[name]))
+
+    def device(self, tower, rows):
+        return {"tower": tower, "rows": rows}
+
+    def along_deep(self, step):
+        return self.device(self.tower, lax.rem(self.deep + step, 4) * 4 + self.flat)
+
+    def along_flat(self, step):
+        return self.device(self.tower, self.deep * 4 + lax.rem(self.flat + step, 4))
+
+
+class Sums:
+    ORDERS = (("c", "x", "z", "y", "w"), ("c", "y", "z", "x", "w"))
+
+    def __init__(self, place, total, landed, out, send_sem, recv_sem, out_sem):
+        self.place, self.total, self.landed, self.out = place, total, landed, out
+        self.send_sem, self.recv_sem, self.out_sem = send_sem, recv_sem, out_sem
+        self.bases = []
+        for order in self.ORDERS:
+            base, bases = 0, [0]
+            for name, half in zip(order, HALVES):
+                base = base + place.bit[name] * half
+                bases.append(base)
+            self.bases.append(bases)
+        self.active = []
+
+    def halve(self, k, unit):
+        order, bases, half = self.ORDERS[unit % 2], self.bases[unit % 2], HALVES[k]
+        name = order[k]
+        start = pl.multiple_of(bases[k] + (1 - self.place.bit[name]) * half, half)
+        return pltpu.make_async_remote_copy(
+            src_ref=self.total.at[unit, pl.ds(start, half)],
+            dst_ref=self.landed.at[unit, pl.ds(OFFSETS[k], half)],
+            send_sem=self.send_sem.at[k, unit],
+            recv_sem=self.recv_sem.at[k, unit],
+            device_id=self.place.to[name],
+            device_id_type=MESH,
+        )
+
+    def own(self, k, unit):
+        return pl.ds(pl.multiple_of(self.bases[unit % 2][k + 1], HALVES[k]), HALVES[k])
+
+    def double(self, k, unit):
+        rows = self.own(k, unit)
+        source = self.total if k == 4 else self.out
+        return pltpu.make_async_remote_copy(
+            src_ref=source.at[unit, rows],
+            dst_ref=self.out.at[unit, rows],
+            send_sem=self.send_sem.at[9 - k, unit],
+            recv_sem=self.recv_sem.at[9 - k, unit],
+            device_id=self.place.to[self.ORDERS[unit % 2][k]],
+            device_id_type=MESH,
+        )
+
+    def keep(self, unit):
+        rows = self.own(4, unit)
+        return pltpu.make_async_copy(
+            self.total.at[unit, rows], self.out.at[unit, rows], self.out_sem.at[unit]
+        )
+
+    def step(self, stage, unit):
+        if 1 <= stage <= 5:
+            k = stage - 1
+            self.halve(k, unit).wait()
+            self.total[unit, self.own(k, unit), :] += self.landed[
+                unit, pl.ds(OFFSETS[k], HALVES[k]), :
+            ]
+        elif stage >= 6:
+            self.double(10 - stage, unit).wait()
+        if stage <= 4:
+            self.halve(stage, unit).start()
+        elif stage <= 9:
+            if stage == 6:
+                self.keep(unit).wait()
+            self.double(9 - stage, unit).start()
+            if stage == 5:
+                self.keep(unit).start()
+
+    def start(self, *units):
+        for unit in units:
+            self.step(0, unit)
+        self.active.append([units, 1])
+
+    def tick(self):
+        for entry in self.active:
+            for unit in entry[0]:
+                self.step(entry[1], unit)
+            entry[1] += 1
+        self.active = [entry for entry in self.active if entry[1] <= 10]
+
+    def finish(self):
+        while self.active:
+            self.tick()
+
+
+class Spread:
+    def __init__(self, place, blocks, send_sem, recv_sem):
+        self.place, self.blocks = place, blocks
+        self.send_sem, self.recv_sem = send_sem, recv_sem
+
+    def copy(self, row, index, where, device):
+        ref = self.blocks.at[where]
+        return pltpu.make_async_remote_copy(
+            src_ref=ref,
+            dst_ref=ref,
+            send_sem=self.send_sem.at[row, index],
+            recv_sem=self.recv_sem.at[row, index],
+            device_id=device,
+            device_id_type=MESH,
+        )
+
+    def copies(self, row, stage):
+        place = self.place
+        if stage == 0:
+            where = (row, place.tower, place.deep, place.flat)
+            return [self.copy(row, i, where, place.along_deep(i + 1)) for i in range(3)]
+        if stage == 1:
+            where = (row, place.tower, slice(None), place.flat)
+            return [self.copy(row, 3 + i, where, place.along_flat(i + 1)) for i in range(3)]
+        return [self.copy(row, 6, (row, place.tower), place.to["c"])]
+
+    def start(self, row, stage):
+        for copy in self.copies(row, stage):
+            copy.start()
+
+    def wait(self, row, stage):
+        for copy in self.copies(row, stage):
+            copy.wait()
+
+
+def layer_kernel(
+    tokens_hbm,
+    segment_ref,
+    positive_ref,
+    gain_one_ref,
+    query_hbm,
+    key_hbm,
+    value_hbm,
+    output_hbm,
+    table_ref,
+    gain_two_ref,
+    inner_hbm,
+    outer_hbm,
+    layer_hbm,
+    token_grad_hbm,
+    sums_hbm,
+    hidden_sum_hbm,
+    rows_grad_hbm,
+    small_ref,
+    tokens,
+    query_w,
+    key_w,
+    value_w,
+    output_w,
+    inner_w,
+    outer_w,
+    normed_one,
+    queries,
+    keys,
+    values,
+    probs,
+    mixed,
+    middle,
+    normed_two,
+    hidden,
+    bias,
+    segment_column,
+    segment_row,
+    pooled_all,
+    hidden_sum,
+    normed_one_t,
+    normed_two_t,
+    mixed_t,
+    grad_mixed,
+    grad_query,
+    grad_key,
+    grad_value,
+    key_total,
+    value_total,
+    total,
+    landed,
+    expand,
+    rounded_grads,
+    small_landed,
+    load_sem,
+    store_sem,
+    sum_send,
+    sum_recv,
+    sum_out,
+    pool_send,
+    pool_recv,
+    hidden_send,
+    hidden_recv,
+    small_send,
+    small_recv,
+):
+    place = Place()
+    barrier = pltpu.get_barrier_semaphore()
+    partners = [place.to["c"]]
+    partners += [place.along_deep(i) for i in (1, 2, 3)]
+    partners += [place.along_flat(i) for i in (1, 2, 3)]
+    for partner in partners:
+        pl.semaphore_signal(barrier, inc=1, device_id=partner, device_id_type=MESH)
+
+    loads = [
+        pltpu.make_async_copy(source, target, load_sem.at[i])
+        for i, (source, target) in enumerate(
+            (
+                (tokens_hbm, tokens),
+                (query_hbm, query_w),
+                (key_hbm, key_w),
+                (value_hbm, value_w),
+                (output_hbm, output_w),
+                (inner_hbm, inner_w),
+                (outer_hbm, outer_w),
+            )
+        )
+    ]
+    for load in loads:
+        load.start()
+
+    segment_row[...] = segment_ref[...].astype(F32)
+    for i in range(8):
+        row = segment_row[i // 4 : i // 4 + 1, (i % 4) * 128 : (i % 4) * 128 + 128]
+        segment_column[i * 128 : (i + 1) * 128, :] = jnp.broadcast_to(row, (128, 128)).T
+    place_row = lax.broadcasted_iota(jnp.int32, (32, FAR), 1)
+    offsets = jnp.where(place_row >= NEAR, place_row - FAR, place_row) - 256
+    by_place = exact_dot(table_ref[...], bucket_onehot(offsets), TN)
+    for h in range(8):
+        spread = jnp.broadcast_to(by_place[h : h + 1], (128, FAR))
+        bias[h] = pltpu.roll(spread, 0, 1, stride=1, stride_axis=0)[:, :NEAR]
+    lane = lax.broadcasted_iota(jnp.int32, (1, 128), 1)
+    item = segment_column[...] + jnp.where(
+        lax.broadcasted_iota(jnp.int32, (1024, 128), 0) >= 512, 8.0, 0.0
+    )
+    item = jnp.where(segment_column[...] < ITEMS_ROW, item, -1.0)
+    slot = jnp.where(lane < 48, lax.rem(lane, 16), -2).astype(F32)
+    expand[...] = jnp.where(item == slot, 1.0, 0.0).astype(BF)
+
+    pooling = Spread(place, pooled_all, pool_send, pool_recv)
+    hiddens = Spread(place, hidden_sum_hbm, hidden_send, hidden_recv)
+    sums = Sums(place, total, landed, sums_hbm, sum_send, sum_recv, sum_out)
+
+    def save_hidden(row):
+        return pltpu.make_async_copy(
+            hidden_sum.at[row],
+            hidden_sum_hbm.at[row, place.tower, place.deep, place.flat],
+            store_sem.at[row],
+        )
+
+    def spread_hidden(row):
+        for i in range(3):
+            yield pltpu.make_async_remote_copy(
+                src_ref=hidden_sum.at[row],
+                dst_ref=hidden_sum_hbm.at[row, place.tower, place.deep, place.flat],
+                send_sem=hidden_send.at[row, i],
+                recv_sem=hidden_recv.at[row, i],
+                device_id=place.along_deep(i + 1),
+                device_id_type=MESH,
+            )
+
+    head_lane = lax.broadcasted_iota(jnp.int32, (1, 256), 1) // 64
+    head_mask = [jnp.where(head_lane == h, 1.0, 0.0) for h in range(4)]
+    head_mask_low = [mask.astype(BF) for mask in head_mask]
+
+    def stack_heads(part):
+        return jnp.concatenate([part * mask for mask in head_mask_low], 0)
+
+    def pick_heads(part):
+        return sum(part[h * 128 : (h + 1) * 128] * head_mask[h] for h in range(4))
+
+    def project(i, carry):
+        rows = tile(i, 256)
+        x = tokens[rows, :].astype(F32)
+        scale = lax.rsqrt(jnp.mean(x * x, axis=1, keepdims=True) + EPSILON)
+        normed = (x * scale * gain_one_ref[...]).astype(BF)
+        normed_one[rows, :] = normed
+        queries[rows, :] = dot(normed, query_w[...]).astype(BF)
+        keys[rows, :] = dot(normed, key_w[...]).astype(BF)
+        values[rows, :] = dot(normed, value_w[...]).astype(BF)
+        return carry
+
+    def window(unit):
+        r, b = lax.div(unit, 4), lax.rem(unit, 4)
+        start = lax.div(b, 2) * 128
+        own = pl.ds(pl.multiple_of(r * 512 + b * 128, 128), 128)
+        near = pl.ds(pl.multiple_of(r * 512 + start, 128), 384)
+        offset = pl.ds(pl.multiple_of(start - 128 * b + 256, 128), 384)
+        return r, own, near, pl.ds(pl.multiple_of(start, 128), 384), offset
+
+    def attend(unit, carry):
+        r, own, near, near_row, offset = window(unit)
+        column = segment_column[own, :]
+        same = jnp.concatenate([column] * 3, 1) == segment_row[pl.ds(r, 1), near_row]
+        for g in range(2):
+            lanes = slice(g * 256, (g + 1) * 256)
+            scores = dot(stack_heads(queries[own, lanes]), keys[near, lanes], NT)
+            parts = []
+            for h in range(4):
+                part = scores[h * 128 : (h + 1) * 128] + bias[g * 4 + h, :, offset]
+                part = jnp.where(same, part, -1e30)
+                highest = jnp.max(part, axis=1, keepdims=True)
+                exp_part = jnp.exp(part - highest)
+                exp_total = jnp.sum(exp_part, axis=1, keepdims=True)
+                parts.append((exp_part * (1.0 / exp_total)).astype(BF))
+            stacked = jnp.concatenate(parts, 0)
+            probs[unit, g] = stacked
+            mixed[own, lanes] = pick_heads(dot(stacked, values[near, lanes])).astype(BF)
+        return carry
+
+    def feed(i, carry):
+        rows = tile(i, 256)
+        branch = dot(mixed[rows, :], output_w[...])
+        mid = tokens[rows, :].astype(F32) + branch
+        middle[rows, :] = mid
+        scale = lax.rsqrt(jnp.mean(mid * mid, axis=1, keepdims=True) + EPSILON)
+        normed = (mid * scale * gain_two_ref[...]).astype(BF)
+        normed_two[rows, :] = normed
+        for c in range(4):
+            lanes = slice(c * 512, (c + 1) * 512)
+            hidden[rows, lanes] = jnp.maximum(dot(normed, inner_w[:, lanes]), 0.0).astype(BF)
+        valid = jnp.where(segment_column[rows, 0:1] < ITEMS_ROW, 1.0, 0.0)
+        small_ref[3:4, :] += jnp.sum(valid * branch * branch, axis=0, keepdims=True)
+        small_ref[5:6, :] += jnp.sum(valid * jnp.ones_like(branch), axis=0, keepdims=True)
+        return carry
+
+    def pool(r):
+        rows = slice(r * 512, (r + 1) * 512)
+        number = lax.broadcasted_iota(jnp.int32, (8, 512), 0).astype(F32)
+        member = jnp.where(segment_row[r : r + 1, :] == number, 1.0, 0.0)
+        member_low = jnp.concatenate([member, jnp.zeros_like(member)], 0).astype(BF)
+        count = jnp.sum(member, axis=1, keepdims=True)
+        hidden_part = dot(member_low, hidden[rows, :])[:8]
+        hidden_sum[r] = hidden_part
+        middle_part = exact_dot(member, middle[rows, :])
+        pieces = split_three(hidden_part)
+        stacked = jnp.concatenate([*pieces, jnp.zeros_like(pieces[0])], 0)
+        branch = dot(stacked, outer_w[...])
+        pooled = (middle_part + (branch[0:8] + branch[8:16] + branch[16:24])) / count
+        sublane = lax.broadcasted_iota(jnp.int32, (8, 128), 0)
+        ids = jnp.zeros((8, 128), F32)
+        for s in range(8):
+            ids = jnp.where(sublane == s, positive_ref[r * 8 + s].astype(F32), ids)
+        lanes = lax.broadcasted_iota(jnp.int32, (8, 128), 1)
+        extra = jnp.where(lanes == 0, ids, count)
+        pooled_all[r, place.tower, place.deep, place.flat] = jnp.concatenate([pooled, extra], 1)
+
+    small_ref[...] = jnp.zeros_like(small_ref)
+    for i in range(4):
+        loads[i].wait()
+    lax.fori_loop(0, 2, project, 0)
+    lax.fori_loop(0, 4, attend, 0)
+    for i in (4, 5):
+        loads[i].wait()
+    lax.fori_loop(0, 2, feed, 0)
+    loads[6].wait()
+    pool(0)
+    pl.semaphore_wait(barrier, len(partners))
+    pooling.start(0, 0)
+    save_hidden(0).start()
+    for copy in spread_hidden(0):
+        copy.start()
+    lax.fori_loop(2, 4, project, 0)
+    pooling.wait(0, 0)
+    pooling.start(0, 1)
+    save_hidden(0).wait()
+    for copy in spread_hidden(0):
+        copy.wait()
+    hiddens.start(0, 1)
+    lax.fori_loop(4, 6, attend, 0)
+    pooling.wait(0, 1)
+    pooling.start(0, 2)
+    lax.fori_loop(6, 8, attend, 0)
+    lax.fori_loop(2, 4, feed, 0)
+    hiddens.wait(0, 1)
+    hiddens.start(0, 2)
+    pool(1)
+    pooling.start(1, 0)
+    save_hidden(1).start()
+
+    def store_rows(source, target, i, index):
+        rows = tile(i, 256)
+        return pltpu.make_async_copy(source.at[rows], target.at[rows], store_sem.at[index])
+
+    def close(i, carry):
+        rows = tile(i, 256)
+        branch = dot(hidden[rows, :], outer_w[...])
+        result = middle[rows, :] + branch
+        grad_query[rows, :] = result.astype(BF)
+        valid = jnp.where(segment_column[rows, 0:1] < ITEMS_ROW, 1.0, 0.0)
+        small_ref[2:3, :] += jnp.sum(valid * result * result, axis=0, keepdims=True)
+        small_ref[4:5, :] += jnp.sum(valid * branch * branch, axis=0, keepdims=True)
+        return carry
+
+    def turn(i, carry):
+        rows = tile(i, 128)
+        normed_two_t[:, rows] = normed_two[rows, :].T
+        mixed_t[:, rows] = mixed[rows, :].T
+        normed_one_t[:, rows] = normed_one[rows, :].T
+        return carry
+
+    lax.fori_loop(0, 4, close, 0)
+    pooling.wait(1, 0)
+    pooling.start(1, 1)
+    save_hidden(1).wait()
+    for copy in spread_hidden(1):
+        copy.start()
+    for i in range(4):
+        store_rows(grad_query, layer_hbm, i, 2 + i).start()
+    lax.fori_loop(0, 8, turn, 0)
+    pooling.wait(1, 1)
+    pooling.start(1, 2)
+    for copy in spread_hidden(1):
+        copy.wait()
+    hiddens.start(1, 1)
+    pooling.wait(0, 2)
+    pooling.wait(1, 2)
+
+    gathered = [
+        jnp.concatenate([pooled_all[r, t].reshape(128, 640) for r in range(2)], 0)
+        for t in range(2)
+    ]
+    vectors, inverse, counts, embedded = [], [], [], []
+    for t in range(2):
+        vector = gathered[t][:, :512]
+        scale = lax.rsqrt(jnp.sum(vector * vector, axis=1, keepdims=True) + EPSILON)
+        vectors.append(vector)
+        inverse.append(scale)
+        embedded.append(vector * scale)
+        counts.append(gathered[t][:, 513:514])
+    logits = exact_dot(embedded[0], embedded[1], NT) / SOFTMAX_TEMP
+    highest = jnp.max(logits, axis=1, keepdims=True)
+    exp_logits = jnp.exp(logits - highest)
+    exp_total = jnp.sum(exp_logits, axis=1, keepdims=True)
+    position = lax.broadcasted_iota(jnp.int32, (256, 256), 1)
+    number = lax.rem(lax.div(position, 8), 16) * 16 + lax.div(position, 128) * 8
+    number = (number + lax.rem(position, 8)).astype(F32)
+    is_target = gathered[0][:, 512:513] == number
+    target = jnp.sum(jnp.where(is_target, logits, 0.0), axis=1, keepdims=True)
+    losses = highest + jnp.log(exp_total) - target
+    loss = jnp.sum(losses, axis=0, keepdims=True) / 256
+    grad_logits = (exp_logits / exp_total - jnp.where(is_target, 1.0, 0.0)) * (LOSS_SCALE / 256)
+    grads = (
+        exact_dot(grad_logits, embedded[1]) / SOFTMAX_TEMP,
+        exact_dot(grad_logits, embedded[0], TN) / SOFTMAX_TEMP,
+    )
+    for t in range(2):
+        along = jnp.sum(grads[t] * embedded[t], axis=1, keepdims=True)
+        per_token = inverse[t] * (grads[t] - embedded[t] * along) / counts[t]
+        for r in range(2):
+            part = per_token[r * 128 : (r + 1) * 128]
+            total[12 + 2 * r + t, 0:128] = part[:, :256]
+            total[12 + 2 * r + t, 128:256] = part[:, 256:]
+            rounded_grads[r, t] = per_token[r * 128 : (r + 1) * 128].astype(BF)
+    save_grads = pltpu.make_async_copy(rounded_grads, rows_grad_hbm, store_sem.at[6])
+    save_grads.start()
+    own_parts = []
+    for r in range(2):
+        spot = 12 + 2 * r + place.tower
+        left, right = tile(place.rows, 8), tile(place.rows + 16, 8)
+        own_parts.append(jnp.concatenate([total[spot, left], total[spot, right]], 1))
+    own = jnp.concatenate(own_parts, 0)
+    pieces = split_three(own)
+    own_low = pieces[0]
+    own_split = jnp.concatenate([*pieces, jnp.zeros((80, 512), BF)], 0)
+
+    def back_hidden(c):
+        lanes = slice(c * 512, (c + 1) * 512)
+        row_part = dot(own_low, outer_w[lanes, :], NT).astype(BF)
+        row_part = jnp.concatenate([row_part, jnp.zeros((112, 512), BF)], 0)
+
+        def mask(i, carry):
+            rows = tile(i, 256)
+            spread = dot(expand[rows, :], row_part)
+            hidden[rows, lanes] = jnp.where(hidden[rows, lanes] > 0, spread, 0.0).astype(BF)
+            return carry
+
+        lax.fori_loop(0, 4, mask, 0)
+        for half in range(2):
+            unit = 2 * c + half
+            total[unit] = dot(normed_two_t[...], hidden[:, unit * 256 : (unit + 1) * 256])
+        sums.start(2 * c, 2 * c + 1)
+
+    def back_middle(i, carry):
+        rows = tile(i, 256)
+        grad_normed = dot(hidden[rows, :], inner_w[...], NT)
+        mid = middle[rows, :]
+        scale = lax.rsqrt(jnp.mean(mid * mid, axis=1, keepdims=True) + EPSILON)
+        small_ref[1:2, :] += jnp.sum(grad_normed * mid * scale, axis=0, keepdims=True)
+        gained = grad_normed * gain_two_ref[...]
+        mean = jnp.mean(gained * mid, axis=1, keepdims=True)
+        grad_mid = dot(expand[rows, :], own_split) + scale * (gained - mid * scale * scale * mean)
+        middle[rows, :] = grad_mid
+        rounded = grad_mid.astype(BF)
+        mixed[rows, :] = rounded
+        grad_mixed[rows, :] = dot(rounded, output_w[...], NT).astype(BF)
+        return carry
+
+    back_hidden(0)
+    back_hidden(1)
+    sums.tick()
+    back_hidden(2)
+    back_hidden(3)
+    sums.tick()
+    lax.fori_loop(0, 4, back_middle, 0)
+    for half in range(2):
+        total[8 + half] = dot(mixed_t[...], mixed[:, half * 256 : (half + 1) * 256])
+    sums.start(8, 9)
+    sums.tick()
+    hiddens.wait(1, 1)
+    hiddens.start(1, 2)
+
+    for i in range(4):
+        store_rows(grad_query, layer_hbm, i, 2 + i).wait()
+    bias[...] = jnp.zeros_like(bias)
+
+    def attend_back(g, unit, carry):
+        r, own, near, near_row, offset = window(unit)
+        lanes = slice(g * 256, (g + 1) * 256)
+        grad_stack = stack_heads(grad_mixed[own, lanes])
+        grad_soft = dot(grad_stack, values[near, lanes], NT)
+        soft = probs[unit, g]
+        parts = []
+        for h in range(4):
+            rows = slice(h * 128, (h + 1) * 128)
+            soft_part = soft[rows].astype(F32)
+            grad_part = grad_soft[rows]
+            along = jnp.sum(soft_part * grad_part, axis=1, keepdims=True)
+            part = (soft_part * (grad_part - along)).astype(BF)
+            bias[g * 4 + h, :, offset] += part.astype(F32)
+            parts.append(part)
+        stacked = jnp.concatenate(parts, 0)
+        grad_query[own, lanes] = pick_heads(dot(stacked, keys[near, lanes])).astype(BF)
+        key_total[near, :] += dot(stacked, stack_heads(queries[own, lanes]), TN)
+        value_total[near, :] += dot(soft, grad_stack, TN)
+        return carry
+
+    for g in range(2):
+        lanes = slice(g * 256, (g + 1) * 256)
+        key_total[...] = jnp.zeros_like(key_total)
+        value_total[...] = jnp.zeros_like(value_total)
+        for quarter in range(4):
+            lax.fori_loop(2 * quarter, 2 * quarter + 2, functools.partial(attend_back, g), 0)
+            sums.tick()
+        grad_key[:, lanes] = key_total[...].astype(BF)
+        grad_value[:, lanes] = value_total[...].astype(BF)
+        total[10 + 3 * g] = dot(normed_one_t[...], grad_query[:, lanes])
+        total[11 + 3 * g] = dot(normed_one_t[...], grad_key[:, lanes])
+        total[12 + 3 * g] = dot(normed_one_t[...], grad_value[:, lanes])
+        sums.start(10 + 3 * g, 11 + 3 * g, 12 + 3 * g)
+
+    def back_tokens(i, carry):
+        rows = tile(i, 256)
+        grad_normed = (
+            dot(grad_query[rows, :], query_w[...], NT)
+            + dot(grad_key[rows, :], key_w[...], NT)
+            + dot(grad_value[rows, :], value_w[...], NT)
+        )
+        x = tokens[rows, :].astype(F32)
+        scale = lax.rsqrt(jnp.mean(x * x, axis=1, keepdims=True) + EPSILON)
+        small_ref[0:1, :] += jnp.sum(grad_normed * x * scale, axis=0, keepdims=True)
+        gained = grad_normed * gain_one_ref[...]
+        mean = jnp.mean(gained * x, axis=1, keepdims=True)
+        grad = middle[rows, :] + scale * (gained - x * scale * scale * mean)
+        normed_one[rows, :] = grad.astype(BF)
+        return carry
+
+    lax.fori_loop(0, 4, back_tokens, 0)
+    for i in range(4):
+        store_rows(normed_one, token_grad_hbm, i, 2 + i).start()
+    mirror = (
+        lax.broadcasted_iota(jnp.int32, (128, 128), 0)
+        + lax.broadcasted_iota(jnp.int32, (128, 128), 1)
+    )
+    mirror = jnp.where(mirror == 127, 1.0, 0.0)
+    diagonals = []
+    for h in range(8):
+        turned = exact_dot(mirror, bias[h])
+        wide = jnp.concatenate([turned, jnp.zeros((128, FAR - NEAR), F32)], 1)
+        wide = pltpu.roll(wide, 0, 1, stride=1, stride_axis=0)
+        diagonals.append(jnp.sum(wide, axis=0, keepdims=True))
+    buckets = exact_dot(jnp.concatenate(diagonals, 0), bucket_onehot(place_row - 383), NT)
+    small_ref[8:16, :] = jnp.concatenate([buckets, jnp.zeros((8, 480), F32)], 1)
+    for i, name in enumerate("cxyzw"):
+        copy = pltpu.make_async_remote_copy(
+            src_ref=small_ref,
+            dst_ref=small_landed.at[i],
+            send_sem=small_send.at[i],
+            recv_sem=small_recv.at[i],
+            device_id=place.to[name],
+            device_id_type=MESH,
+        )
+        copy.start()
+        copy.wait()
+        small_ref[...] += small_landed[i]
+        sums.tick()
+    small_ref[6:7, :] = jnp.broadcast_to(loss, (1, 512))
+    hiddens.wait(0, 2)
+    hiddens.wait(1, 2)
+    save_grads.wait()
+    sums.finish()
+    for i in range(4):
+        store_rows(normed_one, token_grad_hbm, i, 2 + i).wait()
+
+
+def closing_kernel(
+    layer_hbm,
+    token_grad_hbm,
+    sums_hbm,
+    hidden_sum_hbm,
+    rows_grad_ref,
+    small_ref,
+    layer_out,
+    token_out,
+    gain_one_out,
+    query_out,
+    key_out,
+    value_out,
+    output_out,
+    position_out,
+    gain_two_out,
+    inner_out,
+    outer_out,
+    loss_out,
+    square_out,
+    hidden_sum,
+    hidden_low,
+    outer_part,
+    load_sem,
+    copy_sem,
+    store_sem,
+):
+    load = pltpu.make_async_copy(hidden_sum_hbm, hidden_sum, load_sem)
+    load.start()
+    pairs = [(layer_hbm, layer_out), (token_grad_hbm, token_out)]
+    for unit in range(8):
+        pairs.append((sums_hbm.at[unit], inner_out.at[:, pl.ds(unit * 256, 256)]))
+    places = [(output_out, 0), (output_out, 1)]
+    places += [(ref, g) for g in range(2) for ref in (query_out, key_out, value_out)]
+    for unit, (ref, g) in enumerate(places):
+        pairs.append((sums_hbm.at[8 + unit], ref.at[:, pl.ds(g * 256, 256)]))
+    copies = [
+        pltpu.make_async_copy(source, target, copy_sem.at[i])
+        for i, (source, target) in enumerate(pairs)
+    ]
+    for copy in copies:
+        copy.start()
+    gain_one_out[...] = small_ref[0, :]
+    gain_two_out[...] = small_ref[1, :]
+    eye = jnp.where(
+        lax.broadcasted_iota(jnp.int32, (32, 32), 0) == lax.broadcasted_iota(jnp.int32, (32, 32), 1),
+        1.0,
+        0.0,
+    )
+    position_out[...] = exact_dot(eye, small_ref[8:16, 0:32], NT)
+    loss_out[0] = jnp.max(small_ref[6:7, :])
+    squares = jnp.sum(small_ref[2:5, :], axis=1, keepdims=True)
+    valid = jnp.sum(small_ref[5:6, :], axis=1, keepdims=True)
+    roots = jnp.sqrt(squares / valid)
+    for i in range(3):
+        square_out[i] = jnp.max(roots[i : i + 1, :])
+    load.wait()
+    hidden_low[...] = hidden_sum[...].reshape(512, 2048).astype(BF)
+    grads = rows_grad_ref[...].reshape(512, 512)
+    stores = []
+    for c in range(4):
+        if c >= 2:
+            stores[c - 2].wait()
+        outer_part[c % 2] = dot(hidden_low[:, c * 512 : (c + 1) * 512], grads, TN)
+        store = pltpu.make_async_copy(
+            outer_part.at[c % 2], outer_out.at[pl.ds(c * 512, 512)], store_sem.at[c % 2]
+        )
+        store.start()
+        stores.append(store)
+    stores[2].wait()
+    stores[3].wait()
+    for copy in copies:
+        copy.wait()
+
+
+def fast_shards(
+    tokens,
+    segment_ids,
+    positives,
+    attention_gain,
+    query_weight,
+    key_weight,
+    value_weight,
+    output_weight,
+    position_table,
+    feedforward_gain,
+    inner_weight,
+    outer_weight,
+):
+    block_shape = tokens.shape
+    anywhere = pl.BlockSpec(memory_space=pl.ANY)
+    vmem = pl.BlockSpec(memory_space=pltpu.VMEM)
+    smem = pl.BlockSpec(memory_space=pltpu.SMEM)
+    shape = jax.ShapeDtypeStruct
+    dma = pltpu.SemaphoreType.DMA
+    low = functools.partial(pltpu.VMEM, dtype=BF)
+    full = functools.partial(pltpu.VMEM, dtype=F32)
+    outs = pl.pallas_call(
+        layer_kernel,
+        out_shape=[
+            shape((1024, 512), BF),
+            shape((1024, 512), BF),
+            shape((UNITS, 512, 256), F32),
+            shape((2, 2, 4, 4, 8, 2048), F32),
+            shape((2, 2, 128, 512), BF),
+            shape((16, 512), F32),
+        ],
+        in_specs=[anywhere, vmem, smem, vmem]
+        + [anywhere] * 4
+        + [vmem, vmem, anywhere, anywhere],
+        out_specs=[anywhere] * 5 + [vmem],
+        scratch_shapes=[
+            low((1024, 512)),
+            low((512, 512)),
+            low((512, 512)),
+            low((512, 512)),
+            low((512, 512)),
+            low((512, 2048)),
+            low((2048, 512)),
+            low((1024, 512)),
+            low((1024, 512)),
+            low((1024, 512)),
+            low((1024, 512)),
+            low((8, 2, 512, 384)),
+            low((1024, 512)),
+            full((1024, 512)),
+            low((1024, 512)),
+            low((1024, 2048)),
+            full((8, 128, NEAR)),
+            full((1024, 128)),
+            full((2, 512)),
+            full((2, 2, 4, 4, 8, 640)),
+            full((2, 8, 2048)),
+            low((512, 1024)),
+            low((512, 1024)),
+            low((512, 1024)),
+            low((1024, 512)),
+            low((1024, 512)),
+            low((1024, 512)),
+            low((1024, 512)),
+            full((1024, 256)),
+            full((1024, 256)),
+            full((UNITS, 512, 256)),
+            full((UNITS, 496, 256)),
+            low((1024, 128)),
+            low((2, 2, 128, 512)),
+            full((5, 16, 512)),
+            dma((7,)),
+            dma((7,)),
+            dma((10, UNITS)),
+            dma((10, UNITS)),
+            dma((UNITS,)),
+            dma((2, 7)),
+            dma((2, 7)),
+            dma((2, 7)),
+            dma((2, 7)),
+            dma((5,)),
+            dma((5,)),
+        ],
+        compiler_params=pltpu.CompilerParams(
+            collective_id=0, has_side_effects=True, vmem_limit_bytes=63 * 2**20
+        ),
+    )(
+        tokens.reshape(1024, 512),
+        segment_ids.reshape(2, 512),
+        positives,
+        attention_gain.reshape(1, 512),
+        query_weight,
+        key_weight,
+        value_weight,
+        output_weight,
+        position_table,
+        feedforward_gain.reshape(1, 512),
+        inner_weight,
+        outer_weight,
+    )
+    results = pl.pallas_call(
+        closing_kernel,
+        out_shape=[
+            shape((1024, 512), BF),
+            shape((1024, 512), BF),
+            shape((512,), F32),
+            shape((512, 512), F32),
+            shape((512, 512), F32),
+            shape((512, 512), F32),
+            shape((512, 512), F32),
+            shape((32, 8), F32),
+            shape((512,), F32),
+            shape((512, 2048), F32),
+            shape((2048, 512), F32),
+            shape((1,), F32),
+            shape((3,), F32),
+        ],
+        in_specs=[anywhere] * 4 + [vmem, vmem],
+        out_specs=[anywhere, anywhere, vmem]
+        + [anywhere] * 4
+        + [vmem, vmem, anywhere, anywhere, smem, smem],
+        scratch_shapes=[
+            full((2, 2, 4, 4, 8, 2048)),
+            low((512, 2048)),
+            full((2, 512, 512)),
+            dma(()),
+            dma((18,)),
+            dma((2,)),
+        ],
+        compiler_params=pltpu.CompilerParams(vmem_limit_bytes=24 * 2**20),
+    )(*outs)
+    layer, token_grad, *rest = results
+    return (
+        layer.reshape(block_shape),
+        token_grad.reshape(block_shape),
+        *rest[:9],
+        rest[9].reshape(()),
+        rest[10],
+    )
+
+
 def solution(mesh):
+    fast = mesh.shape["tower"] == 2 and mesh.shape["rows"] == 16
     return jax.shard_map(
-        shards,
+        fast_shards if fast else shards,
         mesh=mesh,
         in_specs=(
             P("tower", "rows", None, None),

time: 1500 us -> 196 us (0.13)
  local copies, waits for them, and re-layouts: 1130 us -> 11.8 us
  Pallas kernels: 0 us -> 183 us
  waiting for transfers between devices: 104 us -> 0 us
  matrix products: 95.6 us -> 0 us
  blocking collectives: 83.4 us -> 0 us
  other arithmetic: 51.3 us -> 0 us
  between operations: 17.3 us -> 0.67 us
    gather x2 -> x0, local copies, waits for them, and re-layouts: 937 us -> none  [shards(): jnp.take(position_table.T, jnp.asarray(bucket_index), axis=1)]
    pallas_call x0 -> x2, Pallas kernels: none -> 183 us  [the longest x1 176 us: fast_shards(): pl.pallas_call(layer_kernel, out_shape=[shape((1024, 512), BF), shape((10...]
    dot_general x38 -> x0, matrix products: 95.6 us -> none  [the longest x4 19.9 us: row_scores(): jnp.einsum('qhd,khd->hqk', query_heads, key_heads, preferred_element_type...]
    reduce_scatter x1 -> x0, waiting for transfers between devices: 70.9 us -> none  [shards(): lax.psum_scatter(lax.dot_general(similarity_gradient, my_queries, (((0,),...]
    rev x1 -> x0, local copies, waits for them, and re-layouts: 64.3 us -> none  [diagonal_sums(): flipped = square[:, :, ::-1]]
    unnamed x108 -> x14, local copies, waits for them, and re-layouts: 70.6 us -> 11.8 us
    all_gather x1 -> x0, blocking collectives: 45.4 us -> none  [shards(): lax.all_gather(document_vectors, 'rows', axis=0, tiled=True)]
    psum x1 -> x0, blocking collectives: 38 us -> none  [shards(): lax.psum((attention_gain_grad, query_grad, key_grad, value_grad, output_g...]
  transfers between devices with their start and end apart: 5 -> 0, of which waited for: 4 -> 0; matrix products, arithmetic and copies ran while one was open for 11% -> 0% of each run, Pallas kernels for 0% -> 0%
where the time goes in v1:
time: 196 us
  Pallas kernels  183 us (93%)
  local copies, waits for them, and re-layouts  11.8 us (6%)
    pallas_call x1, Pallas kernels, fast_shards(): pl.pallas_call(layer_kernel, out_shape=[shape((1024, 512), BF), shape((10...  176 us
    unnamed x14, local copies, waits for them, and re-layouts  11.8 us
    pallas_call x1, Pallas kernels, fast_shards(): pl.pallas_call(closing_kernel, out_shape=[shape((1024, 512), BF), shape((...  7.26 us

profile of v1, /device:TPU:0, one launch (start us, length us, event | category | flops | bytes accessed | tf_op | source)
XLA Modules:
  0.0 195.6 jit_solution(899330210304752840)
XLA Ops:
  0.6 1.4 copy.25.table_ref
  2.0 175.8 %shard_map.219 = (bf16[1024,512]{1,0:T(8,128)(2,1)}, bf16[1024,512]{1,0:T(8,128)(2,1)}, f32[16,512,256]{2,1,0:T(8,128)}, f32[2,2,4,4,8,2048]{5,4,3,2,1,0:T(8,128...) custom-call(bf16[1024,512]{1,0:T(8,128)(2,1)} %bitcast.7, s32[2,512]{1,0:T(2,128)} %bitcast.8, s32[16]{0:T(128)} %positive_ref.1, ...), custom_call_target="tpu_custom_call" | custom-call | tf_op jit(solution)/shard_map/pallas_call | solution.py:1136
  177.9 0.0 copy-start
  177.9 3.4 %copy-done = f32[16,512,256]{2,1,0:T(8,128)S(1)} copy-done((f32[16,512,256]{2,1,0:T(8,128)S(1)}, f32[16,512,256]{2,1,0:T(8,128)}, u32[]{:S(2)}) %copy-start) | copy-done | bytes 8388632
  181.2 0.0 copy-start.1
  181.2 2.2 %copy-done.1 = f32[2,2,4,4,8,2048]{5,4,3,2,1,0:T(8,128)S(1)} copy-done((f32[2,2,4,4,8,2048]{5,4,3,2,1,0:T(8,128)S(1)}, f32[2,2,4,4,8,2048]{5,4,3,2,1,0:T(8,128)}, u32[]{:S(2)}) %copy-start.1) | copy-done | bytes 4194328
  183.4 0.0 copy-start.2
  183.4 1.2 copy-done.2
  184.6 0.0 copy-start.3
  184.7 1.2 copy-done.3
  185.9 0.0 copy-start.4
  185.9 1.0 copy-done.4
  186.9 0.0 copy-start.5
  186.9 0.8 copy-done.5
  187.7 7.3 %shard_map.220 = (bf16[1024,512]{1,0:T(8,128)(2,1)}, bf16[1024,512]{1,0:T(8,128)(2,1)}, f32[512]{0:T(512)}, f32[512,512]{1,0:T(8,128)}, f32[512,512]{1,0:T(8,128...) custom-call(bf16[1024,512]{1,0:T(8,128)(2,1)S(1)} %copy-done.2, ...), custom_call_target="tpu_custom_call" | custom-call | tf_op jit(solution)/shard_map/pallas_call | solution.py:1215
  194.9 0.7 copy.26
Async XLA Ops:
  177.9 3.4 %copy-start = (f32[16,512,256]{2,1,0:T(8,128)S(1)}, f32[16,512,256]{2,1,0:T(8,128)}, u32[]{:S(2)}) copy-start(f32[16,512,256]{2,1,0:T(8,128)} %get-tuple-element.34.sums_hbm) | copy-start | bytes 25165828
  181.2 2.2 %copy-start.1 = (f32[2,2,4,4,8,2048]{5,4,3,2,1,0:T(8,128)S(1)}, f32[2,2,4,4,8,2048]{5,4,3,2,1,0:T(8,128)}, u32[]{:S(2)}) copy-start(f32[2,2,4,4,8,2048]{5,4,3,2,1,0:T(8,128)} %get-tuple-element.35.hidden_sum_hbm) | copy-start | bytes 12582916
  183.4 1.2 copy-start.2
  184.6 1.2 copy-start.3
  185.9 1.0 copy-start.4
  186.9 0.8 copy-start.5
